TPU v7x, 32 devices: a whole 2x2x4 slice. The times are simulated.
32 devices in a mesh: rows: 8 (over z, x), cols: 4 (over y, core).
Axes of the slice: x: 2, y: 2, z: 4, core: 2. Of those that a mesh axis runs over, the one named last changes fastest.
Arguments:
- panel_u: bfloat16 [8, 16, 1024, 256], P('rows', 'cols'), may hold values from -2.5 to 2.5
- panel_v: bfloat16 [8, 16, 1024, 256], P('rows', 'cols'), may hold values from -0.1875 to 0.1875
- panel_rank: int32 [8, 16], P('rows', 'cols'), may hold values from 128 to 256
- pivot_u: bfloat16 [2, 16, 1024, 256], P(None, 'cols', 'rows'), may hold values from -2.5 to 2.5
- pivot_v: bfloat16 [2, 16, 1024, 256], P(None, 'cols', 'rows'), may hold values from -0.1875 to 0.1875
- pivot_rank: int32 [2, 16], P(None, 'cols'), may hold values from 128 to 256
- orig_u: bfloat16 [2, 8, 1024, 256], P(None, 'rows'), may hold values from -6 to 6
- orig_v: bfloat16 [2, 8, 1024, 256], P(None, 'rows'), may hold values from -0.375 to 0.375
- sampler: bfloat16 [1024, 256], replicated, may hold values from -6 to 6
Outputs:
- basis: float32 [2, 8, 1024, 256], P(None, 'rows', 'cols')
- coeff: float32 [2, 8, 1024, 256], P(None, 'rows', 'cols')
Inputs may be any that keep to these rules, and one draw needn't show every extreme that they name: `panel_rank`: rank of each panel tile; factor columns at and beyond it carry no weight. `pivot_rank`: rank of each pivot row tile; factor columns at and beyond it carry no weight.
All inputs are finite; a program needn't handle non-finite values.
Results may differ from a plain program's by a relative error of at most 0.012.
Values may be sent and summed in bfloat16 or wider, within the bound.
No kernel may reach another device: no remote copies, remote signals or barrier semaphores. Data moves between devices by JAX's collectives and lax.ppermute only.
A program may use at most 64 MiB of HBM per device.

v0:
```python
import math

import jax
import jax.numpy as jnp
from jax import lax
from jax.sharding import PartitionSpec as P


def rank_mask(ranks, width):
    return (jnp.arange(width, dtype=jnp.int32) < ranks[..., None]).astype(jnp.bfloat16)


def body(panel_u, panel_v, panel_rank, pivot_u, pivot_v, pivot_rank, orig_u, orig_v, sampler):
    order = panel_u.shape[2]
    width = panel_u.shape[3]
    panel_mask = rank_mask(panel_rank, width)
    pivot_mask = rank_mask(pivot_rank, width)
    whole_u, whole_v = (
        lax.all_gather(pivot_u, "rows", axis=2, tiled=True),
        lax.all_gather(pivot_v, "rows", axis=2, tiled=True),
    )
    samp_acc = jnp.einsum("cjnr,ns->cjrs", whole_u, sampler, preferred_element_type=jnp.float32)
    cross_acc = jnp.einsum("ijnr,cjnq->cijrq", panel_v, whole_v, preferred_element_type=jnp.float32)
    sampled = (samp_acc * pivot_mask[..., :, None]).astype(jnp.bfloat16)
    cross = cross_acc.astype(jnp.bfloat16)
    sample_term = jnp.einsum(
        "cijrq,cjqs->cijrs", cross, sampled, preferred_element_type=jnp.float32
    ).astype(jnp.bfloat16)
    sample_term = sample_term * panel_mask[None, :, :, :, None]
    partial_value = -jnp.einsum(
        "ijnr,cijrs->cins", panel_u, sample_term, preferred_element_type=jnp.float32
    )
    share_rows = order // lax.axis_size("cols")
    offset = lax.axis_index("cols") * share_rows
    start_proj = jnp.einsum(
        "cinr,ns->cirs", orig_v, sampler, preferred_element_type=jnp.float32
    ).astype(jnp.bfloat16)
    summed = lax.psum(partial_value.astype(jnp.bfloat16), "cols").astype(jnp.float32)
    ysum = (
        jnp.einsum("cinr,cirs->cins", orig_u, start_proj, preferred_element_type=jnp.float32)
        + summed
    )
    gram = jnp.einsum("cins,cint->cist", ysum, ysum, precision=lax.Precision.HIGHEST)
    factor_low = jnp.linalg.cholesky(gram)
    qfull = lax.linalg.triangular_solve(
        factor_low, ysum, left_side=False, lower=True, transpose_a=True
    )
    qrows = lax.dynamic_slice_in_dim(qfull, offset, share_rows, 2)
    qround = qfull.astype(jnp.bfloat16)
    basis = qrows * math.sqrt(order)
    proj_in = jnp.einsum(
        "ijnr,cins->cijrs", panel_u, qround, preferred_element_type=jnp.float32
    ).astype(jnp.bfloat16)
    proj_in = proj_in * panel_mask[None, :, :, :, None]
    proj_mid = jnp.einsum(
        "cijrq,cijrs->cijqs", cross, proj_in, preferred_element_type=jnp.float32
    ).astype(jnp.bfloat16)
    proj_mid = proj_mid * pivot_mask[:, None, :, :, None]
    terms = -jnp.einsum("cjnq,cijqs->cins", whole_u, proj_mid, preferred_element_type=jnp.float32)
    coeff_part = lax.psum_scatter(
        terms.astype(jnp.bfloat16), "cols", scatter_dimension=2, tiled=True
    ).astype(jnp.float32)
    left_proj = jnp.einsum(
        "cinr,cins->cirs", orig_u, qround, preferred_element_type=jnp.float32
    ).astype(jnp.bfloat16)
    right_rows = lax.dynamic_slice_in_dim(orig_v, offset, share_rows, 2)
    coeff = (
        jnp.einsum("cinr,cirs->cins", right_rows, left_proj, preferred_element_type=jnp.float32)
        + coeff_part
    )
    return (basis, coeff)


def solution(mesh):
    placed = (
        P("rows", "cols", None, None),
        P("rows", "cols", None, None),
        P("rows", "cols"),
        P(None, "cols", "rows", None),
        P(None, "cols", "rows", None),
        P(None, "cols"),
        P(None, "rows", None, None),
        P(None, "rows", None, None),
        P(),
    )
    return jax.shard_map(
        body,
        mesh=mesh,
        in_specs=placed,
        out_specs=(P(None, "rows", "cols", None), P(None, "rows", "cols", None)),
        check_vma=False,
    )
```

profile of v0, /device:TPU:0, one launch (start us, length us, event | category | flops | bytes accessed | tf_op | source)
XLA Modules:
  0.0 382.0 jit_solution(7720489834907330600)
XLA Ops:
  7.2 2.2 copy.28
  9.5 0.7 all-gather.3.cloned.1.call-update
  10.4 78.0 %all-gather.5.cloned.1.call-done = bf16[2,4,1024,256]{2,3,0,1:T(8,128)(2,1)} async-done(((bf16[2,4,128,256]{2,3,0,1:T(8,128)(2,1)}), bf16[2,4,1024,256]{2,3,0,1:T(8,128)(2,1)}) %all-gather.5.cloned.1.call-update) | async-done | bytes 4194320 | tf_op jit(solution)/shard_map/all_gather | solution.py:20
  88.4 5.1 %fusion.20 = bf16[2,4,256,256]{2,3,0,1:T(8,128)(2,1)} fusion(bf16[2,4,1024,256]{2,3,0,1:T(8,128)(2,1)} %all-gather.5.cloned.1.call-done, bf16[1,4,1024,256]{3,2,1,0:T(8,128)(2,1)} %param.10), kind=kOutput, calls=%fused_computation.24 | convolution fusion | flops 1074266112 | bytes 7340032 | tf_op jit(solution)/shard_map/ijnr,cjnq->cijrq/dot_general | solution.py:23
  93.5 68.7 %all-gather.3.cloned.1.call-done = bf16[2,4,1024,256]{3,2,1,0:T(8,128)(2,1)} async-done(((bf16[2,4,128,256]{3,2,1,0:T(8,128)(2,1)}), bf16[2,4,1024,256]{3,2,1,0:T(8,128)(2,1)}) %all-gather.3.cloned.1.call-update) | async-done | bytes 4194320 | tf_op jit(solution)/shard_map/all_gather | solution.py:19
  162.2 5.1 %fusion.39 = bf16[2,4,256,256]{2,3,1,0:T(8,128)(2,1)} fusion(bf16[2,4,256,256]{2,3,0,1:T(8,128)(2,1)} %fusion.20, bf16[2,4,1024,256]{3,2,1,0:T(8,128)(2,1)} %all-gather.3.cloned.1.call-done, f32[2,4,256]{2,1,0:T(4,128)S(1)} %get-tuple-element.28, bf16[1024,256]{1,0:T(8,128)(2,1)S(1)} %copy-done.5, bf16[4,256]{1,0:T(4,128)(2,1)S(1)} %fusion.69), kind=kOutput, calls=%fused_computation.34 | convolution fusion | flops 1345847296 | bytes 6825984 | tf_op jit(solution)/shard_map/cijrq,cjqs->cijrs/dot_general | solution.py:26
  167.2 3.6 fusion.32
  171.0 34.4 %all-reduce.3.cloned.1.call-done = bf16[2,1,1024,256]{2,3,0,1:T(8,128)(2,1)} async-done(((bf16[2,1,1024,256]{2,3,0,1:T(8,128)(2,1)}), bf16[2,1,1024,256]{2,3,0,1:T(8,128)(2,1)}) %all-reduce.3.cloned.1.call-update) | async-done | bytes 1048592 | tf_op jit(solution)/shard_map/psum | solution.py:38
  205.4 3.9 %bitcast_add_fusion = f32[2,1,1024,256]{2,3,0,1:T(8,128)} fusion(bf16[2,1,1024,256]{2,3,0,1:T(8,128)(2,1)} %all-reduce.3.cloned.1.call-done, bf16[2,1,1024,256]{3,2,1,0:T(8,128)(2,1)S(1)} %copy-done.4, bf16[2,1,1024,256]{3,2,1,0:T(8,128)(2,1)} %param.16, bf16[1024,256]{1,0:T(8,128)(2,1)} %param.17), kind=kOutput, calls=%fused_computation.6 | convolution fusion | flops 538050560 | bytes 5767168 | tf_op jit(solution)/shard_map/cinr,cirs->cins/dot_general | solution.py:40
  209.2 4.4 %fusion.3 = f32[2,256,256]{1,2,0:T(8,128)S(1)} fusion(f32[2,1,1024,256]{2,3,0,1:T(8,128)} %bitcast_add_fusion), kind=kOutput, calls=%fused_computation.9 | convolution fusion | flops 1610612736 | bytes 2621440 | tf_op jit(solution)/shard_map/cins,cint->cist/dot_general | solution.py:43
  213.9 0.8 copy-done.3
  214.7 23.6 %custom-call.16 = f32[2,1,128,128]{3,2,1,0:T(8,128)S(1)} custom-call(f32[2,1,128,128]{3,2,1,0:T(8,128)S(1)} %cholesky.125), custom_call_target="Cholesky" | custom-call | tf_op jit(solution)/shard_map/jit(cholesky)/cholesky | solution.py:44
  238.4 19.7 %custom-call.17 = f32[2,1,1,128,128]{3,4,2,1,0:T(8,128)S(1)} custom-call(f32[2,1,1,128,128]{4,3,2,1,0:T(8,128)S(1)} %select_bitcast_fusion), custom_call_target="InvertDiagBlocksLowerTriangular" | custom-call | tf_op jit(solution)/shard_map/jit(cholesky)/cholesky | solution.py:44
  258.1 1.2 bitcast_dynamic-update-slice_fusion.1
  259.3 1.3 fusion.44
  260.6 23.5 %custom-call.18 = f32[2,1,128,128]{3,2,1,0:T(8,128)S(1)} custom-call(f32[2,1,128,128]{3,2,1,0:T(8,128)S(1)} %fusion.44), custom_call_target="Cholesky" | custom-call | tf_op jit(solution)/shard_map/jit(cholesky)/cholesky | solution.py:44
  284.5 5.1 %while.1 = (s32[]{:T(128)}, f32[2,1,256,256]{3,2,1,0:T(8,128)S(1)}, s32[2,2]{1,0:T(2,128)S(1)}, f32[2,2,1,128,128]{4,3,0,2,1:T(8,128)}, s32[]{:T(128)}) while((s32[]{:T(128)}, f32[2,1,256,256]{3,2,1,0:T(8,128)S(1)}, s32[2,2]{1,0:T(2,128)S(1)}, f32[2,2,1,128,128]{4,3,0,2,1:T(8,128)}, s32[]{:T(128)}) %tuple.32), condition=%wide.while_cond, body=%wide.while_body.sunk | while | flops 2 | bytes 263777 | solution.py:45
  284.5 0.6 fusion.89
  285.1 2.0 bitcast_dynamic-update-slice_fusion.3
  287.1 0.6 fusion.89
  287.6 2.0 bitcast_dynamic-update-slice_fusion.3
  289.6 0.8 copy-done.2
  290.4 40.1 %custom-call.19 = f32[2,1,2,128,128]{3,4,2,1,0:T(8,128)S(1)} custom-call(f32[2,1,2,128,128]{4,3,2,1,0:T(8,128)} %bitcast.206), custom_call_target="InvertDiagBlocksLowerTriangular" | custom-call | tf_op jit(solution)/shard_map/triangular_solve | solution.py:45
  330.5 3.2 fusion.78
  333.8 2.0 fusion.37
  335.8 2.3 fusion.77
  338.0 4.1 %fusion.19 = bf16[2,4,256,256]{2,3,1,0:T(8,128)(2,1)} fusion(bf16[1,4,1024,256]{3,2,1,0:T(8,128)(2,1)S(1)} %copy-done, bf16[2,4,256,256]{2,3,0,1:T(8,128)(2,1)} %fusion.20, bf16[2,1024,128]{1,2,0:T(8,128)(2,1)} %get-tuple-element.31, bf16[2,1024,128]{1,2,0:T(8,128)(2,1)} %get-tuple-element.33, bf16[2,4,256]{2,1,0:T(4,128)(2,1)S(1)} %get-tuple-element.27, ...), kind=kOutput, calls=%fused_computation.23 | convolution fusion | flops 1347944448 | bytes 5249024 | tf_op jit(solution)/shard_map/cijrq,cijrs->cijqs/dot_general | solution.py:55
  342.2 4.8 %fusion.35 = bf16[2,1,1024,256]{3,2,0,1:T(8,128)(2,1)} fusion(bf16[2,4,256,256]{2,3,1,0:T(8,128)(2,1)} %fusion.19, bf16[2,4,1024,256]{3,2,1,0:T(8,128)(2,1)} %all-gather.3.cloned.1.call-done), kind=kOutput, calls=%fused_computation.29 | convolution fusion | flops 1074790400 | bytes 6291456 | tf_op jit(solution)/shard_map/cjnq,cijqs->cins/dot_general | solution.py:59
  346.9 1.8 fusion.56
  348.7 2.0 copy.43
  350.8 21.6 %reduce-scatter.2.cloned.1.call-done = bf16[2,1,256,256]{3,2,0,1:T(8,128)(2,1)} async-done(((bf16[2,1,1024,256]{3,2,0,1:T(8,128)(2,1)}), bf16[2,1,256,256]{3,2,0,1:T(8,128)(2,1)}) %reduce-scatter.2.cloned.1.call-update) | async-done | bytes 262160 | tf_op jit(solution)/shard_map/reduce_scatter | solution.py:60
  372.3 3.1 fusion.43
  (40 shorter events, 1.2 us)
Async XLA Ops:
  7.2 160.1 %copy-start = (bf16[1,4,1024,256]{3,2,1,0:T(8,128)(2,1)S(1)}, bf16[1,4,1024,256]{3,2,1,0:T(8,128)(2,1)}, u32[]{:S(2)}) copy-start(bf16[1,4,1024,256]{3,2,1,0:T(8,128)(2,1)} %param.9) | copy-start | bytes 6291460
  7.2 3.1 copy-start.7
  7.2 3.1 copy-start.6
  7.2 81.2 %all-gather.5.cloned.1.call-start = ((), (), s32[]{:S(2)}) async-start(), calls=%async_computation.2 | async-start | bytes 4718592 | tf_op jit(solution)/shard_map/all_gather | solution.py:20
  9.4 152.7 %all-gather.3.cloned.1.call-start = ((), (), s32[]{:S(2)}) async-start(), calls=%async_computation.1 | async-start | bytes 4718592 | tf_op jit(solution)/shard_map/all_gather | solution.py:19
  10.2 195.2 %all-reduce.3.cloned.1.call-start = ((), (), s32[]{:S(2)}) async-start(), calls=%async_computation.3 | async-start | bytes 2097152 | tf_op jit(solution)/shard_map/psum | solution.py:38
  10.4 151.8 %copy-start.5 = (bf16[1024,256]{1,0:T(8,128)(2,1)S(1)}, bf16[1024,256]{1,0:T(8,128)(2,1)}, u32[]{:S(2)}) copy-start(bf16[1024,256]{1,0:T(8,128)(2,1)} %param.17) | copy-start | bytes 1572868
  167.2 38.1 %copy-start.4 = (bf16[2,1,1024,256]{3,2,1,0:T(8,128)(2,1)S(1)}, bf16[2,1,1024,256]{3,2,1,0:T(8,128)(2,1)}, u32[]{:S(2)}) copy-start(bf16[2,1,1024,256]{3,2,1,0:T(8,128)(2,1)} %param.15) | copy-start | bytes 3145732
  170.9 201.5 %reduce-scatter.2.cloned.1.call-start = ((), (), s32[]{:S(2)}) async-start(), calls=%async_computation.4 | async-start | bytes 1310720 | tf_op jit(solution)/shard_map/reduce_scatter | solution.py:60
  213.9 0.8 copy-start.3
  289.6 0.8 copy-start.2
  330.5 3.3 copy-start.1
Sparse Core Ops, SparseCore 0:
  10.7 77.7 all-gather.4
  90.6 71.5 all-gather.2
  171.0 34.3 all-reduce.2
  347.1 25.2 reduce-scatter.1
where the time goes:
time: 382 us
  waiting for transfers between devices  203 us (53%)
  other arithmetic  109 us (29%)
  matrix products  43.9 us (11%)
  between operations  14 us (4%)
  local copies, waits for them, and re-layouts  11.2 us (3%)
    all_gather x1, waiting for transfers between devices, body(): lax.all_gather(pivot_v, 'rows', axis=2, tiled=True)  78 us
    all_gather x1, waiting for transfers between devices, body(): lax.all_gather(pivot_u, 'rows', axis=2, tiled=True)  68.7 us
    another operation x9, other arithmetic, body(): factor_low = jnp.linalg.cholesky(gram)  67 us
    another operation x4, other arithmetic, body(): lax.linalg.triangular_solve(factor_low, ysum, left_side=False, lower=True...  40.3 us
    psum x1, waiting for transfers between devices, body(): lax.psum(partial_value.astype(jnp.bfloat16), 'cols').astype(jnp.float32)  34.4 us
    reduce_scatter x1, waiting for transfers between devices, body(): lax.psum_scatter(terms.astype(jnp.bfloat16), 'cols', scatter_dimension=2,...  21.6 us
  transfers between devices with their start and end apart: 4, of which 4 were waited for; matrix products, arithmetic and copies ran while one was open for 2% of the time, Pallas kernels for 0%

commit v1 on v0

v1 whole, which is shorter than its diff:
```python
import math

import jax
import jax.numpy as jnp
import numpy as np
from jax import lax
from jax.experimental import pallas as pl
from jax.experimental.pallas import tpu as pltpu
from jax.sharding import PartitionSpec as P

F32 = jnp.float32
BF16 = jnp.bfloat16
BLOCK = 32
RING_MOST = 16


def rank_mask(ranks, width):
    return (jnp.arange(width, dtype=jnp.int32) < ranks[..., None]).astype(BF16)


def split3(x):
    high = x.astype(BF16)
    rest = x - high.astype(F32)
    mid = rest.astype(BF16)
    low = (rest - mid.astype(F32)).astype(BF16)
    return high, mid, low


def dot00(a, b):
    return lax.dot_general(a, b, (((0,), (0,)), ((), ())), preferred_element_type=F32)


def dot11(a, b):
    return lax.dot_general(a, b, (((1,), (1,)), ((), ())), preferred_element_type=F32)


def eliminate(panel, first):
    rows, width = panel.shape
    lane = lax.broadcasted_iota(jnp.int32, (1, width), 1)
    sub = lax.broadcasted_iota(jnp.int32, (rows, 1), 0)
    scale = jnp.zeros((rows, 1), F32)
    for k in range(rows):
        here = lane == first + k
        column = panel[:, first + k : first + k + 1]
        pivot = column[k : k + 1, :]
        inverse = 1.0 / pivot
        row = jnp.where(here, 1.0, panel[k : k + 1, :])
        factor = jnp.where(sub > k, column * inverse, 0.0)
        cleared = jnp.where(here & (sub >= k), jnp.where(sub == k, 1.0, 0.0), panel)
        panel = cleared - factor * row
        scale = jnp.where(sub == k, lax.rsqrt(pivot), scale)
    above = (lane > first + sub) & (lane < first + rows)
    return jnp.where(above, 0.0, panel * scale)


def orthonormal(y_ref, q_ref, work):
    width = y_ref.shape[1]
    y = y_ref[...]
    work[...] = lax.dot_general(
        y, y, (((0,), (0,)), ((), ())), precision=lax.Precision.HIGHEST, preferred_element_type=F32
    )
    lane = lax.broadcasted_iota(jnp.int32, (1, width), 1)
    for first in range(0, width, BLOCK):
        last = first + BLOCK
        panel = eliminate(work[first:last, :], first)
        work[first:last, :] = panel
        if last < width:
            high, mid, low = split3(panel)
            left = jnp.concatenate([high, high, mid, mid, high, low], 0)
            right = jnp.concatenate([high, mid, high, mid, low, high], 0)
            update = dot00(left, right)
            inside = (lane >= first) & (lane < last)
            work[last:, :] = jnp.where(inside, 0.0, work[last:, :]) - update[last:, :]
    row = lax.broadcasted_iota(jnp.int32, (width, width), 0)
    col = lax.broadcasted_iota(jnp.int32, (width, width), 1)
    inverse = jnp.where(col <= row, work[...], 0.0)
    m_high, m_low, _ = split3(inverse)
    y_high, y_low, _ = split3(y)
    q_ref[...] = dot11(y_high, m_high) + (dot11(y_high, m_low) + dot11(y_low, m_high))


def cholesky_qr(y):
    rows, width = y.shape
    return pl.pallas_call(
        orthonormal,
        out_shape=jax.ShapeDtypeStruct((rows, width), F32),
        in_specs=[pl.BlockSpec(memory_space=pltpu.VMEM)],
        out_specs=pl.BlockSpec(memory_space=pltpu.VMEM),
        scratch_shapes=[pltpu.VMEM((width, width), F32)],
        compiler_params=pltpu.CompilerParams(vmem_limit_bytes=32 << 20),
        cost_estimate=pl.CostEstimate(flops=20 * rows * width * width, bytes_accessed=8 * rows * width, transcendentals=width),
        name="cholesky_qr",
    )(y)


def ring_order(count):
    if count % 2:
        return list(range(count))
    return list(range(0, count, 2)) + list(range(count - 1, 0, -2))


def ring_gather(block, order, axis):
    count = len(order)
    if count > RING_MOST:
        return [lax.all_gather(block, axis, axis=2, tiled=True)]
    ahead = [(order[(p + 1) % count], order[p]) for p in range(count)]
    behind = [(order[p], order[(p + 1) % count]) for p in range(count)]
    found = {0: block}
    up = down = block
    for step in range(1, (count - 1) // 2 + 1):
        up = lax.ppermute(up, axis, ahead)
        down = lax.ppermute(down, axis, behind)
        found[step] = up
        found[count - step] = down
    if count % 2 == 0:
        half = block.shape[0] // 2
        found[count // 2] = jnp.concatenate(
            [lax.ppermute(up[:half], axis, ahead), lax.ppermute(down[half:], axis, behind)], 0
        )
    return [found[d] for d in range(count)]


def body(panel_u, panel_v, panel_rank, pivot_u, pivot_v, pivot_rank, orig_u, orig_v, sampler):
    order, width = panel_u.shape[2:]
    count = lax.axis_size("rows")
    cols = lax.axis_size("cols")
    pairs = cols // 2
    slab = order // count
    me = lax.axis_index("cols")
    core = me % 2
    pair = me // 2
    swap = [(i, i ^ 1) for i in range(cols)]

    ring = ring_order(count)
    place = np.argsort(np.array(ring))
    table = np.array([[ring[(place[r] + d) % count] for d in range(count)] for r in range(count)], np.int32)
    back = np.argsort(table, axis=1).astype(np.int32)
    row = lax.axis_index("rows")
    sources = jnp.asarray(table)[row]
    natural = jnp.asarray(back)[row]

    panel_mask = rank_mask(panel_rank[0], width)
    pivot_mask = rank_mask(pivot_rank, width)

    blocks_u = ring_gather(pivot_u, ring, "rows")
    blocks_v = ring_gather(pivot_v, ring, "rows")
    whole_u = jnp.concatenate(blocks_u, 2)
    whole_v = jnp.concatenate(blocks_v, 2)

    sampler_ring, panel_v_ring = sampler, panel_v[0]
    if count <= RING_MOST:
        sampler_ring = sampler.reshape(count, slab, -1)[sources].reshape(order, -1)
        panel_v_ring = panel_v[0].reshape(-1, count, slab, width)[:, sources].reshape(-1, order, width)

    sampled = jnp.einsum("cjnr,ns->cjrs", whole_u, sampler_ring, preferred_element_type=F32)
    sampled = (sampled * pivot_mask[..., None]).astype(BF16)
    cross = jnp.einsum("jnr,cjnq->cjrq", panel_v_ring, whole_v, preferred_element_type=F32).astype(BF16)
    sample_term = jnp.einsum("cjrq,cjqs->cjrs", cross, sampled, preferred_element_type=F32).astype(BF16)
    sample_term = sample_term * panel_mask[None, :, :, None]
    update = jnp.einsum("jnr,cjrs->cns", panel_u[0], sample_term, preferred_element_type=F32)

    mine_v = lax.dynamic_index_in_dim(orig_v[:, 0], core, 0, False)
    mine_u = lax.dynamic_index_in_dim(orig_u[:, 0], core, 0, False)
    start_proj = jnp.einsum("nr,ns->rs", mine_v, sampler, preferred_element_type=F32).astype(BF16)
    start = jnp.einsum("nr,rs->ns", mine_u, start_proj, preferred_element_type=F32)

    give = lax.dynamic_index_in_dim(update, 1 - core, 0, False).astype(BF16)
    keep = lax.dynamic_index_in_dim(update, core, 0, False)
    chip = keep + lax.ppermute(give, "cols", swap).astype(F32)
    total = chip
    chip_sent = chip.astype(BF16)
    for shift in range(1, pairs):
        total = total + lax.ppermute(
            chip_sent, "cols", [(i, (i + 2 * shift) % cols) for i in range(cols)]
        ).astype(F32)
    ysum = start - total

    qmine = cholesky_qr(ysum)
    qsent = qmine.astype(BF16)
    qother = lax.ppermute(qsent, "cols", swap)
    qround = jnp.where(core == 0, jnp.stack([qsent, qother]), jnp.stack([qother, qsent]))
    share = order // cols
    rows_mine = lax.dynamic_slice_in_dim(qmine, me * share, share, 0)
    rows_given = lax.dynamic_slice_in_dim(qmine, (me + 1 - 2 * core) * share, share, 0)
    rows_other = lax.ppermute(rows_given, "cols", swap)
    basis = jnp.where(core == 0, jnp.stack([rows_mine, rows_other]), jnp.stack([rows_other, rows_mine]))
    basis = basis * math.sqrt(order)

    proj_in = jnp.einsum("jnr,cns->cjrs", panel_u[0], qround, preferred_element_type=F32).astype(BF16)
    proj_in = proj_in * panel_mask[None, :, :, None]
    proj_mid = jnp.einsum("cjrq,cjrs->cjqs", cross, proj_in, preferred_element_type=F32).astype(BF16)
    proj_mid = proj_mid * pivot_mask[..., None]
    terms = jnp.einsum("cjnq,cjqs->cns", whole_u, proj_mid, preferred_element_type=F32)
    if count <= RING_MOST:
        terms = terms.reshape(-1, count, slab, width)[:, natural]
    terms = terms.reshape(-1, pairs, 2, share, width)
    give = lax.dynamic_index_in_dim(terms, 1 - core, 2, False).astype(BF16)
    keep = lax.dynamic_index_in_dim(terms, core, 2, False)
    chip = keep + lax.ppermute(give, "cols", swap).astype(F32)
    total = lax.dynamic_index_in_dim(chip, pair, 1, False)
    for shift in range(1, pairs):
        sent = lax.dynamic_index_in_dim(chip, (pair + shift) % pairs, 1, False).astype(BF16)
        total = total + lax.ppermute(
            sent, "cols", [(i, (i + 2 * shift) % cols) for i in range(cols)]
        ).astype(F32)

    left_proj = jnp.einsum("cnr,cns->crs", orig_u[:, 0], qround, preferred_element_type=F32).astype(BF16)
    right_rows = lax.dynamic_slice_in_dim(orig_v[:, 0], me * share, share, 1)
    coeff = jnp.einsum("cnr,crs->cns", right_rows, left_proj, preferred_element_type=F32) - total
    return (basis[:, None], coeff[:, None])


def solution(mesh):
    placed = (
        P("rows", "cols", None, None),
        P("rows", "cols", None, None),
        P("rows", "cols"),
        P(None, "cols", "rows", None),
        P(None, "cols", "rows", None),
        P(None, "cols"),
        P(None, "rows", None, None),
        P(None, "rows", None, None),
        P(),
    )
    return jax.shard_map(
        body,
        mesh=mesh,
        in_specs=placed,
        out_specs=(P(None, "rows", "cols", None), P(None, "rows", "cols", None)),
        check_vma=False,
    )
```

time: 382 us -> 194 us (0.51)
  waiting for transfers between devices: 203 us -> 55.4 us
  other arithmetic: 109 us -> 12.5 us
  local copies, waits for them, and re-layouts: 11.2 us -> 46.8 us
  Pallas kernels: 0 us -> 26.2 us
  starting transfers between devices: 0.16 us -> 21.9 us
  matrix products: 43.9 us -> 29.6 us
  between operations: 14 us -> 0.81 us
    all_gather x2 -> x0, waiting for transfers between devices: 147 us -> none  [the longest x1 78 us: body(): lax.all_gather(pivot_v, 'rows', axis=2, tiled=True)]
    another operation x13 -> x1, other arithmetic: 107 us -> 0.9 us  [body(): jnp.stack([qsent, qother])]
    ppermute x0 -> x22, waiting for transfers between devices: none -> 55.4 us  [the longest x6 35.8 us: ring_gather(): up = lax.ppermute(up, axis, ahead)]
    psum x1 -> x0, waiting for transfers between devices: 34.4 us -> none  [body(): lax.psum(partial_value.astype(jnp.bfloat16), 'cols').astype(jnp.float32)]
    pallas_call x0 -> x1, Pallas kernels: none -> 26.2 us  [cholesky_qr(): pl.pallas_call(orthonormal, out_shape=jax.ShapeDtypeStruct((rows, width),...]
    ppermute x0 -> x22, starting transfers between devices: none -> 21.9 us  [the longest x6 12.8 us: ring_gather(): up = lax.ppermute(up, axis, ahead)]
    reduce_scatter x1 -> x0, waiting for transfers between devices: 21.6 us -> none  [body(): lax.psum_scatter(terms.astype(jnp.bfloat16), 'cols', scatter_dimension=2,...]
    unnamed x18 -> x32, local copies, waits for them, and re-layouts: 5.82 us -> 25.7 us
  transfers between devices with their start and end apart: 4 -> 22, of which waited for: 4 -> 11; matrix products, arithmetic and copies ran while one was open for 2% -> 23% of each run, Pallas kernels for 0% -> 0%
where the time goes in v1:
time: 194 us; the launch traced here: 193 us
  waiting for transfers between devices  55.4 us (29%)
  local copies, waits for them, and re-layouts  46.8 us (24%)
  matrix products  29.6 us (15%)
  Pallas kernels  26.2 us (14%)
  starting transfers between devices  21.9 us (11%)
  other arithmetic  12.5 us (6%)
    ppermute x6, waiting for transfers between devices, ring_gather(): up = lax.ppermute(up, axis, ahead)  35.8 us
    pallas_call x1, Pallas kernels, cholesky_qr(): pl.pallas_call(orthonormal, out_shape=jax.ShapeDtypeStruct((rows, width),...  26.2 us
    unnamed x32, local copies, waits for them, and re-layouts  25.7 us
    ppermute x6, starting transfers between devices, ring_gather(): up = lax.ppermute(up, axis, ahead)  12.8 us
    ppermute x1, waiting for transfers between devices, body(): lax.ppermute(chip_sent, 'cols', [(i, (i + 2 * shift) % cols) for i in ran...  10.5 us
    dot_general x1, matrix products, body(): jnp.einsum('cjnq,cjqs->cns', whole_u, proj_mid, preferred_element_type=F32)  5.59 us
    gather x2, local copies, waits for them, and re-layouts, body(): terms = terms.reshape(-1, count, slab, width)[:, natural]  5.36 us
    dot_general x1, matrix products, body(): jnp.einsum('cjrq,cjqs->cjrs', cross, sampled, preferred_element_type=F32)  5.25 us
  transfers between devices with their start and end apart: 22, of which 11 were waited for; matrix products, arithmetic and copies ran while one was open for 23% of the time, Pallas kernels for 0%

profile of v1, /device:TPU:0, one launch (start us, length us, event | category | flops | bytes accessed | tf_op | source)
XLA Modules:
  0.0 193.3 jit_solution(697171534883932524)
XLA Ops:
  2.1 3.0 %collective-permute-start = (bf16[2,4,128,256]{2,3,0,1:T(8,128)(2,1)S(1)}, bf16[2,4,128,256]{2,3,0,1:T(8,128)(2,1)}, u32[]{:S(2)}, u32[]{:S(2)}) collective-permute-start(bf16[2,4,128,256]{2,3,0,1:T(8,128)(2,1)S(1)} %copy.31), channel_id=1, source_target_pairs={{8,0},{16,8},{24,16},{28,24},{20,28},{12,20},{4,12},{0,4},{9,1},{1... | collective-permute-start | bytes 1572872 | tf_op jit(solution)/shard_map/ppermute | solution.py:111
  6.6 1.9 collective-permute-start.8
  9.6 8.5 %collective-permute-done = bf16[2,4,128,256]{2,3,0,1:T(8,128)(2,1)} collective-permute-done((bf16[2,4,128,256]{2,3,0,1:T(8,128)(2,1)S(1)}, bf16[2,4,128,256]{2,3,0,1:T(8,128)(2,1)}, u32[]{:S(2)}, u32[]{:S(2)}) %collective-permute-start) | collective-permute-done | bytes 524320 | tf_op jit(solution)/shard_map/ppermute | solution.py:111
  18.1 2.0 %collective-permute-start.1 = (bf16[2,4,128,256]{2,3,0,1:T(8,128)(2,1)}, bf16[2,4,128,256]{2,3,0,1:T(8,128)(2,1)}, u32[]{:S(2)}, u32[]{:S(2)}) collective-permute-start(bf16[2,4,128,256]{2,3,0,1:T(8,128)(2,1)} %collective-permute-done), channel_id=1, source_target_pairs={{8,0},{16,8},{24,16},{28,24},{20,28},{12,20},{4,12},{0,4},{9,1},{1... | collective-permute-start | bytes 1572872 | tf_op jit(solution)/shard_map/ppermute | solution.py:111
  21.1 8.2 %collective-permute-done.8 = bf16[2,4,128,256]{2,3,1,0:T(8,128)(2,1)} collective-permute-done((bf16[2,4,128,256]{2,3,1,0:T(8,128)(2,1)S(1)}, bf16[2,4,128,256]{2,3,1,0:T(8,128)(2,1)}, u32[]{:S(2)}, u32[]{:S(2)}) %collective-permute-start.8) | collective-permute-done | bytes 524320 | tf_op jit(solution)/shard_map/ppermute | solution.py:111
  29.3 2.0 %collective-permute-start.9 = (bf16[2,4,128,256]{2,3,1,0:T(8,128)(2,1)}, bf16[2,4,128,256]{2,3,1,0:T(8,128)(2,1)}, u32[]{:S(2)}, u32[]{:S(2)}) collective-permute-start(bf16[2,4,128,256]{2,3,1,0:T(8,128)(2,1)} %collective-permute-done.8), channel_id=1, source_target_pairs={{8,0},{16,8},{24,16},{28,24},{20,28},{12,20},{4,12},{0,4},{9,1},{1... | collective-permute-start | bytes 1572872 | tf_op jit(solution)/shard_map/ppermute | solution.py:111
  31.6 9.0 %collective-permute-done.1 = bf16[2,4,128,256]{2,3,0,1:T(8,128)(2,1)} collective-permute-done((bf16[2,4,128,256]{2,3,0,1:T(8,128)(2,1)}, bf16[2,4,128,256]{2,3,0,1:T(8,128)(2,1)}, u32[]{:S(2)}, u32[]{:S(2)}) %collective-permute-start.1) | collective-permute-done | bytes 524320 | tf_op jit(solution)/shard_map/ppermute | solution.py:111
  40.5 2.0 %collective-permute-start.2 = (bf16[2,4,128,256]{2,3,0,1:T(8,128)(2,1)}, bf16[2,4,128,256]{2,3,0,1:T(8,128)(2,1)}, u32[]{:S(2)}, u32[]{:S(2)}) collective-permute-start(bf16[2,4,128,256]{2,3,0,1:T(8,128)(2,1)} %collective-permute-done.1), channel_id=1, source_target_pairs={{8,0},{16,8},{24,16},{28,24},{20,28},{12,20},{4,12},{0,4},{9,1},{1... | collective-permute-start | bytes 1572872 | tf_op jit(solution)/shard_map/ppermute | solution.py:111
  43.4 8.4 %collective-permute-done.9 = bf16[2,4,128,256]{2,3,1,0:T(8,128)(2,1)} collective-permute-done((bf16[2,4,128,256]{2,3,1,0:T(8,128)(2,1)}, bf16[2,4,128,256]{2,3,1,0:T(8,128)(2,1)}, u32[]{:S(2)}, u32[]{:S(2)}) %collective-permute-start.9) | collective-permute-done | bytes 524320 | tf_op jit(solution)/shard_map/ppermute | solution.py:111
  51.8 2.0 %collective-permute-start.10 = (bf16[2,4,128,256]{2,3,1,0:T(8,128)(2,1)}, bf16[2,4,128,256]{2,3,1,0:T(8,128)(2,1)}, u32[]{:S(2)}, u32[]{:S(2)}) collective-permute-start(bf16[2,4,128,256]{2,3,1,0:T(8,128)(2,1)} %collective-permute-done.9), channel_id=1, source_target_pairs={{8,0},{16,8},{24,16},{28,24},{20,28},{12,20},{4,12},{0,4},{9,1},{1... | collective-permute-start | bytes 1572872 | tf_op jit(solution)/shard_map/ppermute | solution.py:111
  53.9 2.0 %gather_fusion = bf16[8,4,128,256]{3,2,1,0:T(8,128)(2,1)} fusion(bf16[4,8,128,256]{3,2,1,0:T(8,128)(2,1)S(1)} %bitcast.118, s32[1024]{0:T(1024)S(1)} %pad_clamp_fusion.1), kind=kCustom, calls=%fused_computation | custom fusion | bytes 4194336 | tf_op jit(solution)/shard_map/gather | solution.py:153
  56.0 3.2 %copy.32 = bf16[4,8,128,256]{3,2,1,0:T(8,128)(2,1)} copy(bf16[4,8,128,256]{3,2,0,1:T(8,128)(2,1)} %bitcast.121) | data formatting | bytes 4194304 | tf_op jit(solution)/shard_map/gather | solution.py:153
  60.5 1.9 %constant_dynamic-update-slice_fusion.5 = bf16[2,4,1024,256]{2,3,0,1:T(8,128)(2,1)} fusion(bf16[2,4,1024,256]{2,3,0,1:T(8,128)(2,1)} %constant_dynamic-update-slice_fusion.6, bf16[2,4,128,256]{2,3,0,1:T(8,128)(2,1)} %collective-permute-done), kind=kLoop, calls=%fused_computation.58 | loop fusion | bytes 1048576
  64.4 1.9 %constant_dynamic-update-slice_fusion.4 = bf16[2,4,1024,256]{2,3,0,1:T(8,128)(2,1)} fusion(bf16[2,4,1024,256]{2,3,0,1:T(8,128)(2,1)} %constant_dynamic-update-slice_fusion.5, bf16[2,4,128,256]{2,3,0,1:T(8,128)(2,1)} %collective-permute-done.1), kind=kLoop, calls=%fused_computation.57 | loop fusion | bytes 1048576
  67.3 2.0 %collective-permute-start.3 = (bf16[1,4,128,256]{2,3,0,1:T(8,128)(2,1)S(1)}, bf16[1,4,128,256]{2,3,0,1:T(8,128)(2,1)S(1)}, u32[]{:S(2)}, u32[]{:S(2)}) collective-permute-start(bf16[1,4,128,256]{2,3,0,1:T(8,128)(2,1)S(1)} %slice.22), channel_id=1, source_target_pairs={{8,0},{16,8},{24,16},{28,24},{20,28},{12,20},{4,12},{0,4},{9,1},{1... | collective-permute-start | bytes 786440 | tf_op jit(solution)/shard_map/ppermute | solution.py:118
  70.4 2.1 %constant_dynamic-update-slice_fusion.11 = bf16[2,4,1024,256]{2,3,1,0:T(8,128)(2,1)} fusion(bf16[2,4,1024,256]{2,3,1,0:T(8,128)(2,1)} %constant_dynamic-update-slice_fusion.12, bf16[2,4,128,256]{2,3,1,0:T(8,128)(2,1)} %collective-permute-done.9), kind=kLoop, calls=%fused_computation.64 | loop fusion | bytes 1048576
  75.2 2.0 %collective-permute-start.11 = (bf16[1,4,128,256]{2,3,1,0:T(8,128)(2,1)S(1)}, bf16[1,4,128,256]{2,3,1,0:T(8,128)(2,1)S(1)}, u32[]{:S(2)}, u32[]{:S(2)}) collective-permute-start(bf16[1,4,128,256]{2,3,1,0:T(8,128)(2,1)S(1)} %slice.24), channel_id=1, source_target_pairs={{8,0},{16,8},{24,16},{28,24},{20,28},{12,20},{4,12},{0,4},{9,1},{1... | collective-permute-start | bytes 786440 | tf_op jit(solution)/shard_map/ppermute | solution.py:118
  82.6 2.0 %constant_dynamic-update-slice_fusion.2 = bf16[2,4,1024,256]{2,3,0,1:T(8,128)(2,1)} fusion(bf16[2,4,1024,256]{2,3,0,1:T(8,128)(2,1)} %maximum_dynamic-update-slice_fusion, bf16[2,4,128,256]{2,3,0,1:T(8,128)(2,1)} %collective-permute-done.6), kind=kLoop, calls=%fused_computation.55 | loop fusion | bytes 1048576
  84.6 1.9 constant_dynamic-update-slice_fusion.1
  86.5 1.9 %constant_dynamic-update-slice_fusion = bf16[2,4,1024,256]{2,3,0,1:T(8,128)(2,1)} fusion(bf16[2,4,1024,256]{2,3,0,1:T(8,128)(2,1)} %constant_dynamic-update-slice_fusion.1, bf16[2,4,128,256]{2,3,0,1:T(8,128)(2,1)} %collective-permute-done.4), kind=kLoop, calls=%fused_computation.53 | loop fusion | bytes 1048576 | tf_op jit(solution)/shard_map/concatenate | solution.py:148
  88.5 4.5 %fusion.10 = bf16[2,4,256,256]{2,3,0,1:T(8,128)(2,1)} fusion(bf16[2,4,1024,256]{2,3,0,1:T(8,128)(2,1)} %constant_dynamic-update-slice_fusion, bf16[4,1024,256,1]{2,1,3,0:T(8,128)(2,1)S(1)} %bitcast.125), kind=kOutput, calls=%fused_computation.13 | convolution fusion | flops 1074266112 | bytes 7340032 | tf_op jit(solution)/shard_map/jnr,cjnq->cjrq/dot_general | solution.py:157
  98.6 5.2 %fusion.11 = bf16[2,4,256,256]{3,2,1,0:T(8,128)(2,1)} fusion(bf16[2,4,1024,256]{2,3,1,0:T(8,128)(2,1)} %constant_dynamic-update-slice_fusion.7, bf16[1024,256,1,1]{1,0,3,2:T(8,128)(2,1)S(1)} %bitcast.126, f32[2,4,256]{2,1,0:T(4,128)S(1)} %get-tuple-element.11, bf16[2,4,256,256]{2,3,0,1:T(8,128)(2,1)} %fusion.10, bf16[4,256]{1,0:T(4,128)(2,1)S(1)} %fusion.47), kind=kOutput, calls=%fused_computation.14 | convolution fusion | flops 1345847296 | bytes 6825984 | tf_op jit(solution)/shard_map/cjrq,cjqs->cjrs/dot_general | solution.py:158
  103.9 3.1 %fusion.4 = f32[2,256,1024]{1,2,0:T(8,128)S(1)} fusion(bf16[2,4,256,256]{3,2,1,0:T(8,128)(2,1)} %fusion.11, bf16[1,4,1024,256]{3,2,1,0:T(8,128)(2,1)} %param.11), kind=kOutput, calls=%fused_computation.8 | convolution fusion | flops 1073741824 | bytes 5242880 | tf_op jit(solution)/shard_map/jnr,cjrs->cns/dot_general | solution.py:160
  110.4 2.3 %fusion.32 = bf16[1024,256]{1,0:T(8,128)(2,1)} fusion(bf16[1024,256]{1,0:T(8,128)(2,1)S(1)} %collective-permute-done.16, f32[2,256,1024]{1,2,0:T(8,128)} %copy-done.2, s32[]{:T(128)S(6)} %select_n.92), kind=kLoop, calls=%fused_computation.35 | loop fusion | flops 786432 | bytes 2097156 | tf_op jit(solution)/shard_map/convert_element_type | solution.py:171
  114.3 2.2 %fusion.24 = f32[1024,256]{1,0:T(8,128)S(1)} fusion(bf16[1024,256]{1,0:T(8,128)(2,1)} %param.19, bf16[2,1,1024,256]{3,2,1,0:T(8,128)(2,1)} %param.18, s32[]{:T(128)S(6)} %select_n.92, bf16[2,1,1024,256]{3,2,1,0:T(8,128)(2,1)} %param.17), kind=kOutput, calls=%fused_computation.23 | convolution fusion | flops 268500992 | bytes 2622464 | tf_op jit(solution)/shard_map/nr,rs->ns/dot_general | solution.py:165
  116.5 10.5 %collective-permute-done.17 = bf16[1024,256]{1,0:T(8,128)(2,1)} collective-permute-done((bf16[1024,256]{1,0:T(8,128)(2,1)}, bf16[1024,256]{1,0:T(8,128)(2,1)}, u32[]{:S(2)}, u32[]{:S(2)}) %collective-permute-start.17) | collective-permute-done | bytes 524320 | tf_op jit(solution)/shard_map/ppermute | solution.py:173
  128.7 26.2 %cholesky_qr.1 = f32[1024,256]{1,0:T(8,128)S(1)} custom-call(f32[1024,256]{1,0:T(8,128)S(1)} %add_subtract_fusion.y_ref), custom_call_target="tpu_custom_call" | custom-call | flops 1342177280 | bytes 2097152 | tf_op jit(solution)/shard_map/cholesky_qr/pallas_call | solution.py:84
  158.0 5.1 %fusion.12 = bf16[2,4,256,256]{3,2,1,0:T(8,128)(2,1)} fusion(bf16[1,4,1024,256]{3,2,1,0:T(8,128)(2,1)} %param.11, bf16[2,4,256,256]{2,3,0,1:T(8,128)(2,1)} %fusion.10, bf16[2,4,256]{2,1,0:T(4,128)(2,1)S(1)} %get-tuple-element.10, bf16[4,256]{1,0:T(4,128)(2,1)S(1)} %fusion.47, bf16[1,1024,256]{2,1,0:T(8,128)(2,1)} %bitcast.28, ...), kind=kOutput, calls=%fused_computation.15 | convolution fusion | flops 1350565888 | bytes 5249025 | tf_op jit(solution)/shard_map/cjrq,cjrs->cjqs/dot_general | solution.py:191
  163.1 5.6 %fusion.60 = f32[2,1024,256,1]{2,1,3,0:T(8,128)} fusion(bf16[2,4,1024,256]{2,3,1,0:T(8,128)(2,1)} %constant_dynamic-update-slice_fusion.7, bf16[2,4,256,256]{3,2,1,0:T(8,128)(2,1)} %fusion.12), kind=kOutput, calls=%fused_computation.89 | convolution fusion | flops 1073741824 | bytes 7340032 | tf_op jit(solution)/shard_map/cjnq,cjqs->cns/dot_general | solution.py:193
  168.7 3.6 %gather_fusion.2 = f32[8,2,128,256]{3,2,1,0:T(8,128)} fusion(f32[2,8,128,256]{3,2,1,0:T(8,128)} %bitcast.119, s32[1024]{0:T(1024)S(1)} %pad_clamp_fusion), kind=kCustom, calls=%fused_computation.2 | custom fusion | bytes 4194336 | tf_op jit(solution)/shard_map/gather | solution.py:195
  184.3 5.1 %collective-permute-done.21 = bf16[2,256,256]{2,1,0:T(8,128)(2,1)} collective-permute-done((bf16[2,256,256]{2,1,0:T(8,128)(2,1)}, bf16[2,256,256]{2,1,0:T(8,128)(2,1)}, u32[]{:S(2)}, u32[]{:S(2)}) %collective-permute-start.21) | collective-permute-done | bytes 262176 | tf_op jit(solution)/shard_map/ppermute | solution.py:203
  189.5 3.8 %fusion.23 = f32[2,1,256,256]{3,2,1,0:T(8,128)} fusion(bf16[2,1,1024,256]{3,2,1,0:T(8,128)(2,1)} %param.17, bf16[2,256,256]{2,1,0:T(8,128)(2,1)} %collective-permute-done.21, f32[2,2,256,256]{3,2,0,1:T(8,128)S(1)} %bitcast_add_fusion.1, s32[]{:T(128)S(6)} %select_n.103, bf16[2,1,1024,256]{3,2,1,0:T(8,128)(2,1)} %param.18, s32[]{:T(128)S(6)} %select_n.96, ...), kind=kOutput, calls=%fused_computation.21 | convolution fusion | flops 337641472 | bytes 3670025 | tf_op jit(solution)/shard_map/cnr,crs->cns/dot_general | solution.py:209
  (81 shorter events, 47.2 us)
Async XLA Ops:
  0.6 53.3 %copy-start = (bf16[1,4,1024,256]{3,2,1,0:T(8,128)(2,1)S(1)}, bf16[1,4,1024,256]{3,2,1,0:T(8,128)(2,1)}, u32[]{:S(2)}) copy-start(bf16[1,4,1024,256]{3,2,1,0:T(8,128)(2,1)} %param.12) | copy-start | bytes 6291460
  0.6 30.8 %copy-start.8 = (s32[1,4]{1,0:T(1,128)S(1)}, s32[1,4]{1,0:T(1,128)}, u32[]{:S(2)}) copy-start(s32[1,4]{1,0:T(1,128)} %param.13) | copy-start | bytes 52
  0.7 30.8 %copy-start.7 = (s32[2,4]{1,0:T(2,128)S(1)}, s32[2,4]{1,0:T(2,128)}, u32[]{:S(2)}) copy-start(s32[2,4]{1,0:T(2,128)} %param.16) | copy-start | bytes 100
  2.1 15.9 %collective-permute-start = (bf16[2,4,128,256]{2,3,0,1:T(8,128)(2,1)S(1)}, bf16[2,4,128,256]{2,3,0,1:T(8,128)(2,1)}, u32[]{:S(2)}, u32[]{:S(2)}) collective-permute-start(bf16[2,4,128,256]{2,3,0,1:T(8,128)(2,1)S(1)} %copy.31), channel_id=1, source_target_pairs={{8,0},{16,8},{24,16},{28,24},{20,28},{12,20},{4,12},{0,4},{9,1},{1... | collective-permute-start | bytes 1572872 | tf_op jit(solution)/shard_map/ppermute | solution.py:111
  5.1 15.0 %collective-permute-start.4 = (bf16[2,4,128,256]{2,3,0,1:T(8,128)(2,1)S(1)}, bf16[2,4,128,256]{2,3,0,1:T(8,128)(2,1)}, u32[]{:S(2)}, u32[]{:S(2)}) collective-permute-start(bf16[2,4,128,256]{2,3,0,1:T(8,128)(2,1)S(1)} %copy.31), channel_id=1, source_target_pairs={{0,8},{8,16},{16,24},{24,28},{28,20},{20,12},{12,4},{4,0},{1,9},{9... | collective-permute-start | bytes 1572872 | tf_op jit(solution)/shard_map/ppermute | solution.py:112
  6.6 22.7 %collective-permute-start.8 = (bf16[2,4,128,256]{2,3,1,0:T(8,128)(2,1)S(1)}, bf16[2,4,128,256]{2,3,1,0:T(8,128)(2,1)}, u32[]{:S(2)}, u32[]{:S(2)}) collective-permute-start(bf16[2,4,128,256]{2,3,1,0:T(8,128)(2,1)S(1)} %copy.35), channel_id=1, source_target_pairs={{8,0},{16,8},{24,16},{28,24},{20,28},{12,20},{4,12},{0,4},{9,1},{1... | collective-permute-start | bytes 1572872 | tf_op jit(solution)/shard_map/ppermute | solution.py:111
  8.5 22.8 %collective-permute-start.12 = (bf16[2,4,128,256]{2,3,1,0:T(8,128)(2,1)S(1)}, bf16[2,4,128,256]{2,3,1,0:T(8,128)(2,1)}, u32[]{:S(2)}, u32[]{:S(2)}) collective-permute-start(bf16[2,4,128,256]{2,3,1,0:T(8,128)(2,1)S(1)} %copy.35), channel_id=1, source_target_pairs={{0,8},{8,16},{16,24},{24,28},{28,20},{20,12},{12,4},{4,0},{1,9},{9... | collective-permute-start | bytes 1572872 | tf_op jit(solution)/shard_map/ppermute | solution.py:112
  18.1 22.5 %collective-permute-start.1 = (bf16[2,4,128,256]{2,3,0,1:T(8,128)(2,1)}, bf16[2,4,128,256]{2,3,0,1:T(8,128)(2,1)}, u32[]{:S(2)}, u32[]{:S(2)}) collective-permute-start(bf16[2,4,128,256]{2,3,0,1:T(8,128)(2,1)} %collective-permute-done), channel_id=1, source_target_pairs={{8,0},{16,8},{24,16},{28,24},{20,28},{12,20},{4,12},{0,4},{9,1},{1... | collective-permute-start | bytes 1572872 | tf_op jit(solution)/shard_map/ppermute | solution.py:111
  20.1 22.5 %collective-permute-start.5 = (bf16[2,4,128,256]{2,3,0,1:T(8,128)(2,1)}, bf16[2,4,128,256]{2,3,0,1:T(8,128)(2,1)}, u32[]{:S(2)}, u32[]{:S(2)}) collective-permute-start(bf16[2,4,128,256]{2,3,0,1:T(8,128)(2,1)} %collective-permute-done.4), channel_id=1, source_target_pairs={{0,8},{8,16},{16,24},{24,28},{28,20},{20,12},{12,4},{4,0},{1,9},{9... | collective-permute-start | bytes 1572872 | tf_op jit(solution)/shard_map/ppermute | solution.py:112
  29.3 22.5 %collective-permute-start.9 = (bf16[2,4,128,256]{2,3,1,0:T(8,128)(2,1)}, bf16[2,4,128,256]{2,3,1,0:T(8,128)(2,1)}, u32[]{:S(2)}, u32[]{:S(2)}) collective-permute-start(bf16[2,4,128,256]{2,3,1,0:T(8,128)(2,1)} %collective-permute-done.8), channel_id=1, source_target_pairs={{8,0},{16,8},{24,16},{28,24},{20,28},{12,20},{4,12},{0,4},{9,1},{1... | collective-permute-start | bytes 1572872 | tf_op jit(solution)/shard_map/ppermute | solution.py:111
  31.3 22.5 %collective-permute-start.13 = (bf16[2,4,128,256]{2,3,1,0:T(8,128)(2,1)}, bf16[2,4,128,256]{2,3,1,0:T(8,128)(2,1)}, u32[]{:S(2)}, u32[]{:S(2)}) collective-permute-start(bf16[2,4,128,256]{2,3,1,0:T(8,128)(2,1)} %collective-permute-done.12), channel_id=1, source_target_pairs={{0,8},{8,16},{16,24},{24,28},{28,20},{20,12},{12,4},{4,0},{1,9},{9... | collective-permute-start | bytes 1572872 | tf_op jit(solution)/shard_map/ppermute | solution.py:112
  40.5 25.8 %collective-permute-start.2 = (bf16[2,4,128,256]{2,3,0,1:T(8,128)(2,1)}, bf16[2,4,128,256]{2,3,0,1:T(8,128)(2,1)}, u32[]{:S(2)}, u32[]{:S(2)}) collective-permute-start(bf16[2,4,128,256]{2,3,0,1:T(8,128)(2,1)} %collective-permute-done.1), channel_id=1, source_target_pairs={{8,0},{16,8},{24,16},{28,24},{20,28},{12,20},{4,12},{0,4},{9,1},{1... | collective-permute-start | bytes 1572872 | tf_op jit(solution)/shard_map/ppermute | solution.py:111
  42.5 26.7 %collective-permute-start.6 = (bf16[2,4,128,256]{2,3,0,1:T(8,128)(2,1)}, bf16[2,4,128,256]{2,3,0,1:T(8,128)(2,1)}, u32[]{:S(2)}, u32[]{:S(2)}) collective-permute-start(bf16[2,4,128,256]{2,3,0,1:T(8,128)(2,1)} %collective-permute-done.5), channel_id=1, source_target_pairs={{0,8},{8,16},{16,24},{24,28},{28,20},{20,12},{12,4},{4,0},{1,9},{9... | collective-permute-start | bytes 1572872 | tf_op jit(solution)/shard_map/ppermute | solution.py:112
  51.8 22.5 %collective-permute-start.10 = (bf16[2,4,128,256]{2,3,1,0:T(8,128)(2,1)}, bf16[2,4,128,256]{2,3,1,0:T(8,128)(2,1)}, u32[]{:S(2)}, u32[]{:S(2)}) collective-permute-start(bf16[2,4,128,256]{2,3,1,0:T(8,128)(2,1)} %collective-permute-done.9), channel_id=1, source_target_pairs={{8,0},{16,8},{24,16},{28,24},{20,28},{12,20},{4,12},{0,4},{9,1},{1... | collective-permute-start | bytes 1572872 | tf_op jit(solution)/shard_map/ppermute | solution.py:111
  53.8 23.5 %collective-permute-start.14 = (bf16[2,4,128,256]{2,3,1,0:T(8,128)(2,1)}, bf16[2,4,128,256]{2,3,1,0:T(8,128)(2,1)S(1)}, u32[]{:S(2)}, u32[]{:S(2)}) collective-permute-start(bf16[2,4,128,256]{2,3,1,0:T(8,128)(2,1)} %collective-permute-done.13), channel_id=1, source_target_pairs={{0,8},{8,16},{16,24},{24,28},{28,20},{20,12},{12,4},{4,0},{1,9},{9... | collective-permute-start | bytes 1572872 | tf_op jit(solution)/shard_map/ppermute | solution.py:112
  53.9 5.2 %copy-start.4 = (bf16[1024,256]{1,0:T(8,128)(2,1)S(1)}, bf16[1024,256]{1,0:T(8,128)(2,1)}, u32[]{:S(2)}) copy-start(bf16[1024,256]{1,0:T(8,128)(2,1)} %param.19) | copy-start | bytes 1572868
  67.3 14.1 %collective-permute-start.3 = (bf16[1,4,128,256]{2,3,0,1:T(8,128)(2,1)S(1)}, bf16[1,4,128,256]{2,3,0,1:T(8,128)(2,1)S(1)}, u32[]{:S(2)}, u32[]{:S(2)}) collective-permute-start(bf16[1,4,128,256]{2,3,0,1:T(8,128)(2,1)S(1)} %slice.22), channel_id=1, source_target_pairs={{8,0},{16,8},{24,16},{28,24},{20,28},{12,20},{4,12},{0,4},{9,1},{1... | collective-permute-start | bytes 786440 | tf_op jit(solution)/shard_map/ppermute | solution.py:118
  70.2 18.2 %copy-start.5 = (bf16[4,8,128,256]{3,2,1,0:T(8,128)(2,1)S(1)}, bf16[4,8,128,256]{3,2,1,0:T(8,128)(2,1)}, u32[]{:S(2)}) copy-start(bf16[4,8,128,256]{3,2,1,0:T(8,128)(2,1)} %copy.32) | copy-start | bytes 6291460
  70.3 11.5 %collective-permute-start.7 = (bf16[1,4,128,256]{2,3,0,1:T(8,128)(2,1)S(1)}, bf16[1,4,128,256]{2,3,0,1:T(8,128)(2,1)S(1)}, u32[]{:S(2)}, u32[]{:S(2)}) collective-permute-start(bf16[1,4,128,256]{2,3,0,1:T(8,128)(2,1)S(1)} %slice.23), channel_id=1, source_target_pairs={{0,8},{8,16},{16,24},{24,28},{28,20},{20,12},{12,4},{4,0},{1,9},{9... | collective-permute-start | bytes 786440 | tf_op jit(solution)/shard_map/ppermute | solution.py:118
  75.2 17.8 %collective-permute-start.11 = (bf16[1,4,128,256]{2,3,1,0:T(8,128)(2,1)S(1)}, bf16[1,4,128,256]{2,3,1,0:T(8,128)(2,1)S(1)}, u32[]{:S(2)}, u32[]{:S(2)}) collective-permute-start(bf16[1,4,128,256]{2,3,1,0:T(8,128)(2,1)S(1)} %slice.24), channel_id=1, source_target_pairs={{8,0},{16,8},{24,16},{28,24},{20,28},{12,20},{4,12},{0,4},{9,1},{1... | collective-permute-start | bytes 786440 | tf_op jit(solution)/shard_map/ppermute | solution.py:118
  77.3 15.8 %collective-permute-start.15 = (bf16[1,4,128,256]{2,3,1,0:T(8,128)(2,1)S(1)}, bf16[1,4,128,256]{2,3,1,0:T(8,128)(2,1)S(1)}, u32[]{:S(2)}, u32[]{:S(2)}) collective-permute-start(bf16[1,4,128,256]{2,3,1,0:T(8,128)(2,1)S(1)} %slice.25), channel_id=1, source_target_pairs={{0,8},{8,16},{16,24},{24,28},{28,20},{20,12},{12,4},{4,0},{1,9},{9... | collective-permute-start | bytes 786440 | tf_op jit(solution)/shard_map/ppermute | solution.py:118
  88.5 10.1 %copy-start.6 = (bf16[8,128,256]{2,1,0:T(8,128)(2,1)S(1)}, bf16[8,128,256]{2,1,0:T(8,128)(2,1)}, u32[]{:S(2)}) copy-start(bf16[8,128,256]{2,1,0:T(8,128)(2,1)} %gather_fusion.1) | copy-start | bytes 1572868
  107.0 1.4 copy-start.2
  108.4 2.0 %collective-permute-start.16 = (bf16[1024,256]{1,0:T(8,128)(2,1)S(1)}, bf16[1024,256]{1,0:T(8,128)(2,1)S(1)}, u32[]{:S(2)}, u32[]{:S(2)}) collective-permute-start(bf16[1024,256]{1,0:T(8,128)(2,1)S(1)} %fusion.33), channel_id=1, source_target_pairs={{0,1},{1,0},{2,3},{3,2},{4,5},{5,4},{6,7},{7,6},{8,9},{9,8},{10,11... | collective-permute-start | bytes 1572872 | tf_op jit(solution)/shard_map/ppermute | solution.py:169
  110.4 2.3 %copy-start.3 = (bf16[1024,256]{1,0:T(8,128)(2,1)}, bf16[1024,256]{1,0:T(8,128)(2,1)S(1)}, u32[]{:S(2)}) copy-start(bf16[1024,256]{1,0:T(8,128)(2,1)S(1)} %collective-permute-done.16) | copy-start | bytes 1572868
  112.7 14.3 %collective-permute-start.17 = (bf16[1024,256]{1,0:T(8,128)(2,1)}, bf16[1024,256]{1,0:T(8,128)(2,1)}, u32[]{:S(2)}, u32[]{:S(2)}) collective-permute-start(bf16[1024,256]{1,0:T(8,128)(2,1)} %fusion.32), channel_id=1, source_target_pairs={{0,2},{1,3},{2,0},{3,1},{4,6},{5,7},{6,4},{7,5},{8,10},{9,11},{10,... | collective-permute-start | bytes 1572872 | tf_op jit(solution)/shard_map/ppermute | solution.py:173
  155.8 2.3 %collective-permute-start.19 = (bf16[1024,256]{1,0:T(8,128)(2,1)}, bf16[1024,256]{1,0:T(8,128)(2,1)}, u32[]{:S(2)}, u32[]{:S(2)}) collective-permute-start(bf16[1024,256]{1,0:T(8,128)(2,1)} %convert_element_type.104), channel_id=1, source_target_pairs={{0,1},{1,0},{2,3},{3,2},{4,5},{5,4},{6,7},{7,6},{8,9},{9,8},{10,11... | collective-permute-start | bytes 1572872 | tf_op jit(solution)/shard_map/ppermute | solution.py:180
  174.1 1.4 copy-start.1
  176.3 2.3 %collective-permute-start.20 = (bf16[2,2,256,256]{3,2,0,1:T(8,128)(2,1)}, bf16[2,2,256,256]{3,2,0,1:T(8,128)(2,1)}, u32[]{:S(2)}, u32[]{:S(2)}) collective-permute-start(bf16[2,2,256,256]{3,2,0,1:T(8,128)(2,1)} %fusion.34), channel_id=1, source_target_pairs={{0,1},{1,0},{2,3},{3,2},{4,5},{5,4},{6,7},{7,6},{8,9},{9,8},{10,11... | collective-permute-start | bytes 1572872 | tf_op jit(solution)/shard_map/ppermute | solution.py:199
  177.2 5.3 %collective-permute-start.18 = (f32[256,256]{1,0:T(8,128)}, f32[256,256]{1,0:T(8,128)}, u32[]{:S(2)}, u32[]{:S(2)}) collective-permute-start(f32[256,256]{1,0:T(8,128)} %get-tuple-element.9), channel_id=1, source_target_pairs={{0,1},{1,0},{2,3},{3,2},{4,5},{5,4},{6,7},{7,6},{8,9},{9,8},{10,11... | collective-permute-start | bytes 786440 | tf_op jit(solution)/shard_map/ppermute | solution.py:185
  180.8 8.7 %collective-permute-start.21 = (bf16[2,256,256]{2,1,0:T(8,128)(2,1)}, bf16[2,256,256]{2,1,0:T(8,128)(2,1)}, u32[]{:S(2)}, u32[]{:S(2)}) collective-permute-start(bf16[2,256,256]{2,1,0:T(8,128)(2,1)} %fusion.43), channel_id=1, source_target_pairs={{0,2},{1,3},{2,0},{3,1},{4,6},{5,7},{6,4},{7,5},{8,10},{9,11},{10,... | collective-permute-start | bytes 786440 | tf_op jit(solution)/shard_map/ppermute | solution.py:203
